TPU v7x, 256 devices: a whole 4x4x8 slice. The times are simulated.
256 devices in a mesh: dp: 4 (over y), seq: 64 (over x, z, core).
Axes of the slice: x: 4, y: 4, z: 8, core: 2. Of those that a mesh axis runs over, the one named last changes fastest.
Arguments:
- hidden_in: bfloat16 [65536, 2048], P(('dp', 'seq')), parts along dimension 0, may hold values from -6 to 6
- lin_query: bfloat16 [65536, 1024], P(('dp', 'seq')), parts along dimension 0, may hold values from -6 to 6
- lin_key: bfloat16 [65536, 256], P(('dp', 'seq')), parts along dimension 0, may hold values from -6 to 6
- lin_value: bfloat16 [65536, 256], P(('dp', 'seq')), parts along dimension 0, may hold values from -6 to 6
- lin_gain: float32 [1024], replicated, may hold values from 0.1 to 1.9
- lin_out_weight: bfloat16 [1024, 2048], replicated, may hold values from -0.1875 to 0.1875
- soft_gain: float32 [2048], replicated, may hold values from 0.1 to 1.9
- soft_wq: bfloat16 [2048, 1024], replicated, may hold values from -4 to 4
- soft_wk: bfloat16 [2048, 256], replicated, may hold values from -4 to 4
- soft_wv: bfloat16 [2048, 256], replicated, may hold values from -0.125 to 0.125
- pattern: int32 [2, 128, 18], replicated, may hold values from 0 to 127, as said below
Outputs:
- attended: bfloat16 [65536, 1024], P(('dp', 'seq')), parts along dimension 0
There are 4 independent parts, one for each index of `dp`. A program takes and returns all parts, laid end to end along the dimension named above; an argument that names none is the same for every part. Nothing has to cross between parts.
Inputs may be any that keep to these rules, and one draw needn't show every extreme that they name: pattern[g, b, 0] = b and pattern[g, b, 1] = max(b - 1, 0); every entry of row b lies between 0 and b; for each key-value head and the 2 query blocks held by one device, the entries in slots 2 to 17 of those rows that lie in another device's tokens all name the same key block of that device.
All inputs are finite; a program needn't handle non-finite values.
Results may differ from a plain program's by a relative error of at most 0.035.
Values may be sent and summed in bfloat16 or wider, within the bound.
A program may use at most 128 MiB of HBM per device.

v0:
```python
import jax
import jax.numpy as jnp
from jax import lax
from jax.sharding import PartitionSpec as P

HEAD_DIM = 128
HEADS = 8
KV_HEADS = 2
BLOCK = 128


EPSILON = 1e-06


def carried_in(shard, axis, combine, identity):
    devices, position = (lax.axis_size(axis), lax.axis_index(axis))
    everything = lax.all_gather(shard, axis)
    start = jnp.broadcast_to(jnp.asarray(identity, shard.dtype), shard.shape)

    def lap(k, before):
        reached = k < position
        new = combine(before, everything[k])
        return jnp.where(reached, new, before)

    return lax.fori_loop(0, devices, lap, start)


def add_states(earlier, later):
    return earlier + later


def local(
    hidden_in,
    lin_query,
    lin_key,
    lin_value,
    lin_gain,
    lin_out_weight,
    soft_gain,
    soft_wq,
    soft_wk,
    soft_wv,
    pattern,
):
    tok_count = hidden_in.shape[0]
    local_blocks = tok_count // BLOCK
    per_group = HEADS // KV_HEADS
    listed = pattern.shape[2]
    position = lax.axis_index("seq")
    query_blocks = lin_query.reshape(local_blocks, BLOCK, KV_HEADS, per_group, HEAD_DIM)
    key_blocks = lin_key.reshape(local_blocks, BLOCK, KV_HEADS, HEAD_DIM)
    value_blocks = lin_value.reshape(local_blocks, BLOCK, KV_HEADS, HEAD_DIM)
    block_states = jnp.einsum(
        "ntgd,ntge->ngde", key_blocks, value_blocks, preferred_element_type=jnp.float32
    )
    device_state = jnp.sum(block_states, axis=0)
    carried = carried_in(device_state, "seq", add_states, jnp.zeros_like(device_state))
    running = jnp.concatenate(
        [jnp.zeros_like(block_states[:1]), jnp.cumsum(block_states[:-1], axis=0)], axis=0
    )
    before = carried[None] + running
    inter = jnp.einsum(
        "ntgpd,ngde->ntgpe",
        query_blocks.astype(jnp.float32),
        before,
        precision=lax.Precision.HIGHEST,
    )
    rows_here = jnp.arange(BLOCK)
    causal = rows_here[:, None] >= rows_here[None, :]
    local_scores = jnp.einsum(
        "ntgpd,nsgd->ngpts", query_blocks, key_blocks, preferred_element_type=jnp.float32
    )
    local_scores = jnp.where(causal, local_scores, 0.0).astype(jnp.bfloat16)
    intra = jnp.einsum(
        "ngpts,nsge->ntgpe", local_scores, value_blocks, preferred_element_type=jnp.float32
    )
    mixed = (inter + intra).reshape(tok_count, HEADS, HEAD_DIM)
    normed = (
        mixed
        * lax.rsqrt(jnp.mean(mixed * mixed, axis=-1, keepdims=True) + EPSILON)
        * lin_gain.reshape(HEADS, HEAD_DIM)
    )
    normed = normed.reshape(tok_count, HEADS * HEAD_DIM).astype(jnp.bfloat16)
    branch = jnp.dot(normed, lin_out_weight, preferred_element_type=jnp.float32)
    residual = (hidden_in.astype(jnp.float32) + branch).astype(jnp.bfloat16)
    widened = residual.astype(jnp.float32)
    layer_in = (
        widened
        * lax.rsqrt(jnp.mean(widened * widened, axis=-1, keepdims=True) + EPSILON)
        * soft_gain
    ).astype(jnp.bfloat16)
    soft_query = jnp.dot(layer_in, soft_wq, preferred_element_type=jnp.float32).astype(jnp.bfloat16)
    soft_key = jnp.dot(layer_in, soft_wk, preferred_element_type=jnp.float32).astype(jnp.bfloat16)
    soft_value = jnp.dot(layer_in, soft_wv, preferred_element_type=jnp.float32).astype(jnp.bfloat16)
    packed = jnp.concatenate(
        [
            soft_key.reshape(tok_count, KV_HEADS, HEAD_DIM),
            soft_value.reshape(tok_count, KV_HEADS, HEAD_DIM),
        ],
        axis=-1,
    )
    mine = lax.dynamic_slice_in_dim(pattern, position * local_blocks, local_blocks, 1)
    whole = lax.all_gather(packed, "seq", axis=0, tiled=True)
    table = whole.reshape(-1, BLOCK, KV_HEADS, 2 * HEAD_DIM)
    group_ids = jnp.arange(KV_HEADS)[:, None, None]
    tiles = table[mine, :, group_ids, :]
    tiles = tiles.reshape(KV_HEADS, local_blocks, listed * BLOCK, 2 * HEAD_DIM)
    keys_tile = tiles[..., :HEAD_DIM]
    values_tile = tiles[..., HEAD_DIM:]
    soft_blocks = soft_query.reshape(local_blocks, BLOCK, KV_HEADS, per_group, HEAD_DIM)
    scores = jnp.einsum(
        "ntgpd,gnkd->gnptk", soft_blocks, keys_tile, preferred_element_type=jnp.float32
    ) * HEAD_DIM ** (-0.5)
    same = mine[..., :, None] == mine[..., None, :]
    earlier = jnp.arange(listed)[None, :] < jnp.arange(listed)[:, None]
    repeated = jnp.any(same & earlier, axis=-1)
    live = jnp.repeat(jnp.logical_not(repeated), BLOCK, axis=-1)
    columns = jnp.arange(listed * BLOCK)
    causal_keys = (columns[None, :] >= BLOCK) | (columns[None, :] <= rows_here[:, None])
    allowed = live[:, :, None, None, :] & causal_keys[None, None, None]
    highest = jnp.max(jnp.where(allowed, scores, -jnp.inf), axis=-1, keepdims=True)
    weights = jnp.where(allowed, jnp.exp(scores - highest), 0.0)
    total = jnp.sum(weights, axis=-1, keepdims=True)
    probs = (weights / total).astype(jnp.bfloat16)
    attended = jnp.einsum(
        "gnptk,gnke->ntgpe", probs, values_tile, preferred_element_type=jnp.float32
    )
    return attended.reshape(tok_count, HEADS * HEAD_DIM).astype(jnp.bfloat16)


def solution(mesh):
    in_specs = (
        P(("dp", "seq"), None),
        P(("dp", "seq"), None),
        P(("dp", "seq"), None),
        P(("dp", "seq"), None),
        P(),
        P(),
        P(),
        P(),
        P(),
        P(),
        P(),
    )
    out_specs = P(("dp", "seq"), None)
    return jax.shard_map(local, mesh=mesh, in_specs=in_specs, out_specs=out_specs, check_vma=False)
```

profile of v0, /device:TPU:1, one launch (start us, length us, event | category | flops | bytes accessed | tf_op | source)
XLA Modules:
  0.0 329.4 jit_solution(11226672005344907080)
XLA Ops:
  6.5 1.0 reshape.120
  9.5 1.4 reshape.122
  10.9 86.4 %all-gather.6.cloned.1.call-done = f32[128,128,128]{2,1,0:T(8,128)} async-done(((f32[2,128,128]{2,1,0:T(8,128)}), f32[128,128,128]{2,1,0:T(8,128)}) %all-gather.6.cloned.1.call-update) | async-done | bytes 8388624 | tf_op jit(solution)/shard_map/all_gather | solution.py:17
  97.4 62.3 %while.14 = (s32[]{:T(128)}, f32[2,128,128]{2,1,0:T(8,128)S(1)}, s32[]{:T(128)}, f32[64,2,128,128]{3,2,1,0:T(8,128)}, s32[]{:T(128)}, /*index=5*/s32[]{:T(128)}) while((s32[]{:T(128)}, f32[2,128,128]{2,1,0:T(8,128)S(1)}, s32[]{:T(128)}, f32[64,2,128,128]{3,2,1,0:T(8,128)}, s32[]{:T(128)}, /*index=5*/s32[]{:T(128)}) %tuple.44), condition=%wide.region_2.3_spmd.clone, body=%wide.region_1.2_spmd.clone.sunk | while | flops 98308 | bytes 393317 | solution.py:25
  98.4 0.9 add_select_fusion.2
  99.3 0.9 add_select_fusion.2
  100.3 0.9 add_select_fusion.2
  101.3 0.9 add_select_fusion.2
  102.2 0.9 add_select_fusion.2
  103.2 0.9 add_select_fusion.2
  104.2 0.9 add_select_fusion.2
  105.2 0.9 add_select_fusion.2
  106.1 0.9 add_select_fusion.2
  107.1 0.9 add_select_fusion.2
  108.1 0.9 add_select_fusion.2
  109.1 0.9 add_select_fusion.2
  110.0 0.9 add_select_fusion.2
  111.0 0.9 add_select_fusion.2
  112.0 0.9 add_select_fusion.2
  113.0 0.9 add_select_fusion.2
  113.9 0.9 add_select_fusion.2
  114.9 0.9 add_select_fusion.2
  115.9 0.9 add_select_fusion.2
  116.9 0.9 add_select_fusion.2
  117.8 0.9 add_select_fusion.2
  118.8 0.9 add_select_fusion.2
  119.8 0.9 add_select_fusion.2
  120.7 0.9 add_select_fusion.2
  121.7 0.9 add_select_fusion.2
  122.7 0.9 add_select_fusion.2
  123.7 0.9 add_select_fusion.2
  124.6 0.9 add_select_fusion.2
  125.6 0.9 add_select_fusion.2
  126.6 0.9 add_select_fusion.2
  127.6 0.9 add_select_fusion.2
  128.5 0.9 add_select_fusion.2
  129.5 0.9 add_select_fusion.2
  130.5 0.9 add_select_fusion.2
  131.5 0.9 add_select_fusion.2
  132.4 0.9 add_select_fusion.2
  133.4 0.9 add_select_fusion.2
  134.4 0.9 add_select_fusion.2
  135.4 0.9 add_select_fusion.2
  136.3 0.9 add_select_fusion.2
  137.3 0.9 add_select_fusion.2
  138.3 0.9 add_select_fusion.2
  139.2 0.9 add_select_fusion.2
  140.2 0.9 add_select_fusion.2
  141.2 0.9 add_select_fusion.2
  142.2 0.9 add_select_fusion.2
  160.3 1.5 multiply_reduce_fusion
  161.9 1.7 copy.85
  164.4 3.9 %fusion.13 = (f32[256]{0:T(256)S(1)}, bf16[256,2048]{1,0:T(8,128)(2,1)S(1)}) fusion(bf16[1024,2048]{1,0:T(8,128)(2,1)} %param.18, f32[256,1024]{1,0:T(8,128)S(1)} %reshape.123, f32[32,8,8,128]{3,2,1,0:T(8,128)S(1)} %bitcast.81, f32[1024]{0:T(1024)S(1)} %copy-done.4, bf16[256,2048]{1,0:T(8,128)(2,1)} %param.13), kind=kOutput, calls=%fused_computation.24 | convolution fusion | flops 1077673728 | bytes 8393728 | tf_op jit(solution)/shard_map/dot_general | solution.py:84
  169.4 2.2 convolution_convert_fusion.2
  173.3 1.2 fusion.29
  174.5 1.7 broadcast_and_fusion
  176.3 3.8 %convolution_convert_fusion = bf16[256,1024]{1,0:T(8,128)(2,1)S(1)} fusion(bf16[2048,1024]{1,0:T(8,128)(2,1)} %param.20, bf16[256,2048]{1,0:T(8,128)(2,1)} %copy-done.5, f32[2048]{0:T(1024)S(1)} %copy-done.3, f32[256]{0:T(256)S(1)} %add_rsqrt_fusion.1), kind=kOutput, calls=%fused_computation.34 | convolution fusion | flops 1076101120 | bytes 5776384 | tf_op jit(solution)/shard_map/dot_general | solution.py:92
  180.4 89.2 %all-gather.4.cloned.1.call-done = bf16[16384,2,256]{2,0,1:T(8,128)(2,1)} async-done(((bf16[256,2,256]{2,0,1:T(8,128)(2,1)}), bf16[16384,2,256]{2,0,1:T(8,128)(2,1)}) %all-gather.4.cloned.1.call-update) | async-done | bytes 16777232 | tf_op jit(solution)/shard_map/all_gather | solution.py:103
  269.6 14.0 %copy.90 = bf16[128,128,2,256]{3,1,2,0:T(8,128)(2,1)} copy(bf16[128,128,2,256]{3,1,0,2:T(8,128)(2,1)} %bitcast.76) | data formatting | bytes 33554432 | tf_op jit(solution)/shard_map/reshape | solution.py:104
  283.6 12.9 %gather_fusion = bf16[72,128,256]{2,1,0:T(8,128)(2,1)} fusion(bf16[128,128,2,256]{3,1,2,0:T(8,128)(2,1)} %copy.90, s32[72]{0:T(128)S(1)} %reshape.129), kind=kCustom, calls=%fused_computation | custom fusion | bytes 9437760 | tf_op jit(solution)/shard_map/gather | solution.py:106
  296.5 4.3 %fusion.11 = f32[2,2,2304,128,4]{3,2,4,1,0:T(8,128)S(1)} fusion(bf16[2,2,2304,256]{3,2,1,0:T(8,128)(2,1)} %bitcast.77, bf16[2,128,2,4,128]{4,3,2,1,0:T(4,128)(2,1)S(1)} %reshape.128), kind=kOutput, calls=%fused_computation.20 | convolution fusion | flops 1207959552 | bytes 21757952 | tf_op jit(solution)/shard_map/ntgpd,gnkd->gnptk/dot_general | solution.py:111
  300.8 11.6 %fusion.64 = (f32[2,2,4,128]{3,2,1,0:T(4,128)S(1)}, f32[2,2,4,128,2304]{3,4,2,1,0:T(8,128)}) fusion(f32[2,2,2304,128,4]{3,2,4,1,0:T(8,128)S(1)} %fusion.11, pred[2,2,128,2304]{2,3,1,0:T(8,128)(4,1)S(1)} %broadcast_and_fusion), kind=kOutput, calls=%fused_computation.76 | output fusion | flops 28313856 | bytes 38936576 | tf_op jit(solution)/shard_map/sub | solution.py:122
  312.3 8.8 %fusion.24 = bf16[2,128,2,4,128]{1,4,3,2,0:T(8,128)(2,1)S(1)} fusion(f32[2,2,4,128,2304]{3,4,2,1,0:T(8,128)} %get-tuple-element.117, f32[2,2,4,128]{3,2,1,0:T(4,128)S(1)} %get-tuple-element.116, bf16[2,2,2304,256]{3,2,1,0:T(8,128)(2,1)} %bitcast.78), kind=kOutput, calls=%fused_computation.35 | convolution fusion | flops 1217658880 | bytes 21766144 | tf_op jit(solution)/shard_map/gnptk,gnke->ntgpe/dot_general | solution.py:125
  321.4 1.2 convert_element_type.52
  (62 shorter events, 23.9 us)
Async XLA Ops:
  6.5 161.8 %copy-start = (bf16[2048,256]{1,0:T(8,128)(2,1)S(1)}, bf16[2048,256]{1,0:T(8,128)(2,1)}, u32[]{:S(2)}) copy-start(bf16[2048,256]{1,0:T(8,128)(2,1)} %param.22) | copy-start | bytes 3145732
  6.5 90.8 %all-gather.6.cloned.1.call-start = ((), (), s32[]{:S(2)}) async-start(), calls=%async_computation.1 | async-start | bytes 8519680 | tf_op jit(solution)/shard_map/all_gather | solution.py:17
  9.4 260.2 %all-gather.4.cloned.1.call-start = ((), (), s32[]{:S(2)}) async-start(), calls=%async_computation | async-start | bytes 17039360 | tf_op jit(solution)/shard_map/all_gather | solution.py:103
  159.7 4.7 %copy-start.4 = (f32[1024]{0:T(1024)S(1)}, f32[1024]{0:T(1024)}, u32[]{:S(2)}) copy-start(f32[1024]{0:T(1024)} %param.17) | copy-start | bytes 12292
  164.4 4.0 %copy-start.3 = (f32[2048]{0:T(1024)S(1)}, f32[2048]{0:T(1024)}, u32[]{:S(2)}) copy-start(f32[2048]{0:T(1024)} %param.19) | copy-start | bytes 24580
  168.3 1.0 copy-start.5
  168.3 4.2 %copy-start.2 = (s32[2,128,18]{1,0,2:T(2,128)S(1)}, s32[2,128,18]{1,0,2:T(2,128)}, u32[]{:S(2)}) copy-start(s32[2,128,18]{1,0,2:T(2,128)} %param.23) | copy-start | bytes 55300
  312.3 10.3 %copy-start.1 = (bf16[2048,256]{1,0:T(8,128)(2,1)S(1)}, bf16[2048,256]{1,0:T(8,128)(2,1)}, u32[]{:S(2)}) copy-start(bf16[2048,256]{1,0:T(8,128)(2,1)} %param.22) | copy-start | bytes 3145732
Sparse Core Ops, SparseCore 0:
  10.1 87.1 all-gather.5
  172.6 96.9 all-gather.3
where the time goes:
time: 331 us; the launch traced here: 329 us
  waiting for transfers between devices  176 us (53%)
  other arithmetic  76.4 us (23%)
  local copies, waits for them, and re-layouts  35.5 us (11%)
  matrix products  26.7 us (8%)
  between operations  13.7 us (4%)
    all_gather x1, waiting for transfers between devices, local(): whole = lax.all_gather(packed, 'seq', axis=0, tiled=True)  89.2 us
    all_gather x1, waiting for transfers between devices, carried_in(): everything = lax.all_gather(shard, axis)  86.4 us
    select_n x64, other arithmetic, lap(): return jnp.where(reached, new, before)  60.8 us
    reshape x1, local copies, waits for them, and re-layouts, local(): table = whole.reshape(-1, BLOCK, KV_HEADS, 2 * HEAD_DIM)  14 us
    gather x1, local copies, waits for them, and re-layouts, local(): tiles = table[mine, :, group_ids, :]  12.9 us
    sub x1, other arithmetic, local(): weights = jnp.where(allowed, jnp.exp(scores - highest), 0.0)  11.6 us
    dot_general x1, matrix products, local(): jnp.einsum('gnptk,gnke->ntgpe', probs, values_tile, preferred_element_typ...  8.79 us
  transfers between devices with their start and end apart: 2, of which 2 were waited for; matrix products, arithmetic and copies ran while one was open for 3% of the time, Pallas kernels for 0%

commit v1 on v0

v1 whole, which is shorter than its diff:
```python
import math

import jax
import jax.numpy as jnp
from jax import lax
from jax.experimental import pallas as pl
from jax.experimental.pallas import tpu as pltpu
from jax.sharding import PartitionSpec as P

HEAD_DIM = 128
HEADS = 8
KV_HEADS = 2
PER_GROUP = HEADS // KV_HEADS
BLOCK = 128
SEL = 18
TOK = 256
D = 2048
NX, NZ = 4, 8
CHIP_TOK = 2 * TOK
PAIRS = SEL // 2
EPSILON = 1e-06
NEG = -1e30
COEF = HEAD_DIM ** (-0.5) * math.log2(math.e)
F32, BF16 = jnp.float32, jnp.bfloat16
MESH = pl.DeviceIdType.MESH

ROWS_A = 208
ROWS_B = CHIP_TOK - ROWS_A
ORDER = [(0, 0), (0, 1), (1, 1), (0, 2), (1, 2), (0, 3), (1, 3), (0, 4)]


def dot(a, b):
    return jnp.dot(a, b, preferred_element_type=F32)


def dot_nt(a, b):
    return lax.dot_general(a, b, (((1,), (1,)), ((), ())), preferred_element_type=F32)


def dot_tn(a, b):
    return lax.dot_general(a, b, (((0,), (0,)), ((), ())), preferred_element_type=F32)


def kernel(
    pattern, lin_gain, soft_gain, hidden_hbm, lq_hbm, lk_hbm, lv_hbm, wo_hbm, wq_hbm, wk_hbm, wv_hbm,
    o_ref,
    hidden, lq, lk, lv, wo, wq, wkv, st_send, st_recv, tot_send, tot_recv, pre_send, pre_recv,
    block0, lin_scores, normed, resid, layer_in, kv_send, q_send, q_all, table, scores, bias, o_send, o_all,
    load_sem, st_ssem, st_rsem, tot_ssem, tot_rsem, pre_ssem, pre_rsem, sib_ssem, sib_rsem,
    a1_ssem, a1_rsem, a2_ssem, a2_rsem, b1_ssem, b1_rsem, b2_ssem, b2_rsem,
):
    me = lax.axis_index("seq")
    core = lax.rem(me, 2)
    chip = me // 2
    z = lax.rem(chip, NZ)
    x = chip // NZ
    sign = 1 - 2 * core
    row_pos = z * 2 + core

    def dev(cx, cz, cc):
        return {"seq": (lax.rem(cx + 2 * NX, NX) * NZ + lax.rem(cz + 2 * NZ, NZ)) * 2 + cc}

    sibling = dev(x, z, 1 - core)

    def remote(src, dst, ssem, rsem, device):
        return pltpu.make_async_remote_copy(
            src_ref=src, dst_ref=dst, send_sem=ssem, recv_sem=rsem, device_id=device, device_id_type=MESH
        )

    barrier = pltpu.get_barrier_semaphore()
    for i in range(1, 2 * NZ):
        pos = lax.rem(row_pos + i, 2 * NZ)
        pl.semaphore_signal(barrier, inc=1, device_id={"seq": x * 2 * NZ + pos}, device_id_type=MESH)
    for i in range(1, NX):
        pl.semaphore_signal(barrier, inc=1, device_id=dev(x + i, z, core), device_id_type=MESH)

    own_q = pl.ds(pl.multiple_of(core * 512, 512), 512)
    sib_q = pl.ds(pl.multiple_of((1 - core) * 512, 512), 512)
    own_h = pl.ds(pl.multiple_of(core * 128, 128), 128)
    sib_h = pl.ds(pl.multiple_of((1 - core) * 128, 128), 128)
    loads = [
        (lk_hbm, lk),
        (lv_hbm, lv),
        (lq_hbm, lq),
        (wo_hbm, wo),
        (hidden_hbm, hidden),
        (wk_hbm.at[:, own_h], wkv.at[0, :, 0:128]),
        (wv_hbm.at[:, own_h], wkv.at[0, :, 128:256]),
        (wk_hbm.at[:, sib_h], wkv.at[1, :, 0:128]),
        (wv_hbm.at[:, sib_h], wkv.at[1, :, 128:256]),
        (wq_hbm.at[:, own_q], wq.at[0]),
        (wq_hbm.at[:, sib_q], wq.at[1]),
    ]
    loads = [pltpu.make_async_copy(src, dst, load_sem.at[i]) for i, (src, dst) in enumerate(loads)]
    for copy in loads:
        copy.start()
    loads[0].wait()
    loads[1].wait()

    for g in range(KV_HEADS):
        cols = slice(g * 128, g * 128 + 128)
        first = dot_tn(lk[0:128, cols], lv[0:128, cols])
        second = dot_tn(lk[128:256, cols], lv[128:256, cols])
        block0[g] = first
        st_send[g] = (first + second).reshape(NZ, 16, 128)

    pl.semaphore_wait(barrier, 2 * NZ - 1 + NX - 1)

    st_copies = []
    for i in range(1, 2 * NZ):
        pos = lax.rem(row_pos + i, 2 * NZ)
        copy = remote(
            st_send.at[lax.rem(pos, 2), pos // 2], st_recv.at[row_pos], st_ssem.at[i - 1], st_rsem.at[i - 1],
            {"seq": x * 2 * NZ + pos},
        )
        copy.start()
        st_copies.append(copy)
    st_recv[row_pos] = st_send[core, z]

    loads[2].wait()
    tri = lax.broadcasted_iota(jnp.int32, (128, 128), 0) >= lax.broadcasted_iota(jnp.int32, (128, 128), 1)
    tri4 = jnp.concatenate([tri] * PER_GROUP, axis=0)

    def stacked(n, g):
        return jnp.concatenate(
            [lq[n * 128 : n * 128 + 128, (g * PER_GROUP + h) * 128 : (g * PER_GROUP + h) * 128 + 128] for h in range(PER_GROUP)],
            axis=0,
        )

    for n in range(2):
        for g in range(KV_HEADS):
            keys = lk[n * 128 : n * 128 + 128, g * 128 : g * 128 + 128]
            lin_scores[n, g] = jnp.where(tri4, dot_nt(stacked(n, g), keys), 0.0).astype(BF16)

    for copy in st_copies:
        copy.wait()
    total = st_recv[0]
    for i in range(1, 2 * NZ):
        total = total + st_recv[i]
    tot_send[...] = total
    tot_copies = []
    for i in range(1, NX):
        copy = remote(tot_send, tot_recv.at[i - 1], tot_ssem.at[i - 1], tot_rsem.at[i - 1], dev(x + i, z, core))
        copy.start()
        tot_copies.append(copy)
    for copy in tot_copies:
        copy.wait()
    running = jnp.zeros((16, 128), F32)
    for i in range(1, NX):
        running = running + jnp.where(x - i >= 0, tot_recv[i - 1], 0.0)
    for i in range(2 * NZ):
        pre_send[i] = running
        running = running + st_recv[i]
    pre_copies = []
    for i in range(1, 2 * NZ):
        pos = lax.rem(row_pos + i, 2 * NZ)
        copy = remote(
            pre_send.at[pos], pre_recv.at[core, z], pre_ssem.at[i - 1], pre_rsem.at[i - 1], {"seq": x * 2 * NZ + pos}
        )
        copy.start()
        pre_copies.append(copy)
    pre_recv[core, z] = pre_send[row_pos]
    for copy in pre_copies:
        copy.wait()

    for n in range(2):
        for g in range(KV_HEADS):
            state = pre_recv[g].reshape(128, 128)
            if n == 1:
                state = state + block0[g]
            high = state.astype(BF16)
            low = (state - high.astype(F32)).astype(BF16)
            qs = stacked(n, g)
            mix = dot(
                jnp.concatenate([qs, qs, lin_scores[n, g]], axis=1),
                jnp.concatenate([high, low, lv[n * 128 : n * 128 + 128, g * 128 : g * 128 + 128]], axis=0),
            )
            mix = mix * lax.rsqrt(jnp.mean(mix * mix, axis=-1, keepdims=True) + EPSILON)
            for h in range(PER_GROUP):
                cols = slice((g * PER_GROUP + h) * 128, (g * PER_GROUP + h) * 128 + 128)
                normed[n * 128 : n * 128 + 128, cols] = (mix[h * 128 : h * 128 + 128] * lin_gain[:, cols]).astype(BF16)

    loads[3].wait()
    loads[4].wait()
    squares = jnp.zeros((TOK, 128), F32)
    for t in range(4):
        cols = slice(t * 512, t * 512 + 512)
        res = (hidden[:, cols].astype(F32) + dot(normed[...], wo[:, cols])).astype(BF16)
        resid[:, cols] = res
        wide = res.astype(F32)
        wide = wide * wide
        for s in range(4):
            squares = squares + wide[:, s * 128 : s * 128 + 128]
    factor = lax.rsqrt(jnp.sum(squares, axis=-1, keepdims=True) * (1.0 / D) + EPSILON)
    for t in range(4):
        cols = slice(t * 512, t * 512 + 512)
        layer_in[:, cols] = (resid[:, cols].astype(F32) * factor * soft_gain[:, cols]).astype(BF16)

    for i in range(5, 9):
        loads[i].wait()
    flat = table.reshape(NX * NZ * CHIP_TOK, 256)
    my_rows = pl.ds(pl.multiple_of(me * TOK, TOK), TOK)
    kv_send[...] = dot(layer_in[...], wkv[1]).astype(BF16)
    kv_copy = remote(kv_send, flat.at[my_rows], sib_ssem.at[0], sib_rsem.at[0], sibling)
    kv_copy.start()
    flat[my_rows] = dot(layer_in[...], wkv[0]).astype(BF16)
    kv_copy.wait()

    rows_a, rows_b = (0, ROWS_A), (ROWS_A, ROWS_B)
    pending = []

    def send(src_chip, rows, ssem, rsem, device):
        part = flat.at[pl.ds(pl.multiple_of(src_chip * CHIP_TOK + rows[0], 16), rows[1])]
        copy = remote(part, part, ssem, rsem, device)
        copy.start()
        pending.append(copy)
        return copy

    def row_chip(direction, distance):
        step = -sign if direction == 0 else sign
        return x * NZ + lax.rem(z + step * distance + NZ, NZ)

    def col_chip(cx, cz):
        return lax.rem(cx + NX, NX) * NZ + lax.rem(cz + NZ, NZ)

    def z_dev(direction):
        return dev(x, z + (sign if direction == 0 else -sign), core)

    a1 = [send(chip, rows_a, a1_ssem.at[i - 1], a1_rsem.at[i - 1], dev(x + i, z, core)) for i in (1, 3, 2)]
    b1 = {}
    b2 = {}

    def send_b1(direction, t):
        b1[direction, t] = send(
            row_chip(direction, t - 1), rows_b, b1_ssem.at[direction, t - 1], b1_rsem.at[direction, t - 1], z_dev(direction)
        )

    def send_b2(r):
        src = row_chip(*ORDER[r])
        for j, dx in enumerate((1, -1)):
            b2[r, j] = send(src, rows_b, b2_ssem.at[r, j], b2_rsem.at[r, j], dev(x + dx, z, core))

    def forward_b2(r):
        j = r % 2
        b2[r, j].wait_recv()
        direction, distance = ORDER[r]
        step = -sign if direction == 0 else sign
        src = col_chip(x + (-1 if j == 0 else 1), z + step * distance)
        b2[r, 2] = send(src, rows_b, b2_ssem.at[r, 2], b2_rsem.at[r, 2], dev(x + (1 if j == 0 else -1), z, core))

    a2 = {}

    def send_a2(direction, t):
        step = -sign if direction == 0 else sign
        for i in range(NX):
            src = col_chip(x + i, z + step * (t - 1))
            a2[direction, t, i] = send(
                src, rows_a, a2_ssem.at[direction, t - 1, i], a2_rsem.at[direction, t - 1, i], z_dev(direction)
            )

    send_b1(0, 1)
    send_b1(1, 1)
    send_b2(0)

    loads[9].wait()
    loads[10].wait()

    def put_queries(part, write):
        q = dot(layer_in[...], wq[part]).astype(BF16)
        for n in range(2):
            for h in range(PER_GROUP):
                write(n, h, q[n * 128 : n * 128 + 128, h * 128 : h * 128 + 128])

    def write_send(n, h, value):
        q_send[n, h * 128 : h * 128 + 128, :] = value

    def write_own(n, h, value):
        q_all[core * 2 + n, h * 128 : h * 128 + 128, :] = value

    put_queries(1, write_send)
    q_copy = remote(q_send, q_all.at[pl.ds(core * 2, 2)], sib_ssem.at[1], sib_rsem.at[1], sibling)
    q_copy.start()

    for copy in a1:
        copy.wait_recv()
    send_a2(0, 1)
    send_a2(1, 1)
    put_queries(0, write_own)

    def find_repeats(i, carry):
        entries = [pattern[core, chip * 4 + i, j] for j in range(SEL)]
        for j in range(SEL):
            value = jnp.float32(0.0)
            for e in range(j):
                value = jnp.where(entries[e] == entries[j], jnp.float32(NEG), value)
            bias[i, j] = value
        return carry

    lax.fori_loop(0, 4, find_repeats, 0)

    b1[0, 1].wait_recv()
    send_b1(0, 2)
    send_b2(1)
    b1[1, 1].wait_recv()
    send_b1(1, 2)
    send_b2(2)
    forward_b2(0)
    b1[0, 2].wait_recv()
    send_b1(0, 3)
    send_b2(3)
    b1[1, 2].wait_recv()
    send_b1(1, 3)
    send_b2(4)
    forward_b2(1)
    b1[0, 3].wait_recv()
    send_b1(0, 4)
    send_b2(5)
    b1[1, 3].wait_recv()
    send_b2(6)
    forward_b2(2)
    b1[0, 4].wait_recv()
    send_b2(7)
    for i in range(NX):
        a2[0, 1, i].wait_recv()
    send_a2(0, 2)
    for i in range(NX):
        a2[1, 1, i].wait_recv()
    send_a2(1, 2)
    forward_b2(3)
    forward_b2(4)
    for i in range(NX):
        a2[0, 2, i].wait_recv()
    send_a2(0, 3)
    for i in range(NX):
        a2[1, 2, i].wait_recv()
    send_a2(1, 3)
    forward_b2(5)
    forward_b2(6)
    for i in range(NX):
        a2[0, 3, i].wait_recv()
    send_a2(0, 4)
    forward_b2(7)
    for i in range(NX):
        a2[1, 3, i].wait_recv()
        a2[0, 4, i].wait_recv()
    for r in range(NZ):
        b2[r, 1 - r % 2].wait_recv()
        b2[r, 2].wait_recv()
    q_copy.wait()
    for copy in pending:
        copy.wait_send()

    def block_of(i, j):
        return pattern[core, chip * 4 + i, j]

    def attend(part, n):
        i = (1 - core if part == 0 else core) * 2 + n
        q = q_all[i]
        top = jnp.full((512, 128), NEG, F32)
        for p in range(PAIRS):
            keys = jnp.concatenate([table[block_of(i, 2 * p)][:, 0:128], table[block_of(i, 2 * p + 1)][:, 0:128]], axis=0)
            s = dot_nt(q, keys) * COEF
            left, right = s[:, 0:128] + bias[i, 2 * p], s[:, 128:256] + bias[i, 2 * p + 1]
            if p == 0:
                left = jnp.where(tri4, left, NEG)
            scores[p, :, 0:128] = left
            scores[p, :, 128:256] = right
            top = jnp.maximum(top, jnp.maximum(left, right))
        top = jnp.max(top, axis=-1, keepdims=True)
        total = jnp.zeros((512, 128), F32)
        out = jnp.zeros((512, 128), F32)
        for p in range(PAIRS):
            values = jnp.concatenate([table[block_of(i, 2 * p)][:, 128:256], table[block_of(i, 2 * p + 1)][:, 128:256]], axis=0)
            w = jnp.exp2(scores[p] - top)
            total = total + (w[:, 0:128] + w[:, 128:256])
            out = out + dot(w.astype(BF16), values)
        out = (out / jnp.sum(total, axis=-1, keepdims=True)).astype(BF16)
        rows = pl.ds(pl.multiple_of(n * 128, 128), 128)
        for h in range(PER_GROUP):
            if part == 0:
                o_send[rows, h * 128 : h * 128 + 128] = out[h * 128 : h * 128 + 128]
            else:
                o_all[core, rows, h * 128 : h * 128 + 128] = out[h * 128 : h * 128 + 128]

    @pl.loop(0, 2)
    def _(n):
        attend(0, n)

    o_copy = remote(o_send, o_all.at[core], sib_ssem.at[2], sib_rsem.at[2], sibling)
    o_copy.start()

    @pl.loop(0, 2)
    def _(n):
        attend(1, n)

    o_copy.wait()
    o_ref[:, 0:512] = o_all[0]
    o_ref[:, 512:1024] = o_all[1]


def local(hidden_in, lin_query, lin_key, lin_value, lin_gain, lin_out_weight, soft_gain, soft_wq, soft_wk, soft_wv, pattern):
    dma = pltpu.SemaphoreType.DMA
    vmem, anywhere = pl.BlockSpec(memory_space=pltpu.VMEM), pl.BlockSpec(memory_space=pl.ANY)
    scratch = [
        pltpu.VMEM((TOK, D), BF16),
        pltpu.VMEM((TOK, 1024), BF16),
        pltpu.VMEM((TOK, 256), BF16),
        pltpu.VMEM((TOK, 256), BF16),
        pltpu.VMEM((1024, D), BF16),
        pltpu.VMEM((2, D, 512), BF16),
        pltpu.VMEM((2, D, 256), BF16),
        pltpu.VMEM((2, NZ, 16, 128), F32),
        pltpu.VMEM((2 * NZ, 16, 128), F32),
        pltpu.VMEM((16, 128), F32),
        pltpu.VMEM((NX - 1, 16, 128), F32),
        pltpu.VMEM((2 * NZ, 16, 128), F32),
        pltpu.VMEM((2, NZ, 16, 128), F32),
        pltpu.VMEM((2, 128, 128), F32),
        pltpu.VMEM((2, 2, 512, 128), BF16),
        pltpu.VMEM((TOK, 1024), BF16),
        pltpu.VMEM((TOK, D), BF16),
        pltpu.VMEM((TOK, D), BF16),
        pltpu.VMEM((TOK, 256), BF16),
        pltpu.VMEM((2, 512, 128), BF16),
        pltpu.VMEM((4, 512, 128), BF16),
        pltpu.VMEM((NX * NZ * CHIP_TOK // BLOCK, BLOCK, 256), BF16),
        pltpu.VMEM((PAIRS, 512, 256), F32),
        pltpu.SMEM((4, SEL), F32),
        pltpu.VMEM((TOK, 512), BF16),
        pltpu.VMEM((2, TOK, 512), BF16),
        dma((11,)),
        dma((2 * NZ - 1,)), dma((2 * NZ - 1,)),
        dma((NX - 1,)), dma((NX - 1,)),
        dma((2 * NZ - 1,)), dma((2 * NZ - 1,)),
        dma((3,)), dma((3,)),
        dma((3,)), dma((3,)),
        dma((2, 4, NX)), dma((2, 4, NX)),
        dma((2, 4)), dma((2, 4)),
        dma((NZ, 3)), dma((NZ, 3)),
    ]
    return pl.pallas_call(
        kernel,
        name="mixer_and_attention",
        out_shape=jax.ShapeDtypeStruct((TOK, 1024), BF16),
        in_specs=[pl.BlockSpec(memory_space=pltpu.SMEM), vmem, vmem] + [anywhere] * 8,
        out_specs=vmem,
        scratch_shapes=scratch,
        compiler_params=pltpu.CompilerParams(collective_id=0, has_side_effects=True, vmem_limit_bytes=56 << 20),
    )(
        pattern, lin_gain.reshape(1, 1024), soft_gain.reshape(1, D),
        hidden_in, lin_query, lin_key, lin_value, lin_out_weight, soft_wq, soft_wk, soft_wv,
    )


def solution(mesh):
    whole, split = P(), P(("dp", "seq"), None)
    in_specs = (split, split, split, split) + (whole,) * 7
    return jax.shard_map(local, mesh=mesh, in_specs=in_specs, out_specs=split, check_vma=False)
```

time: 331 us -> 107 us (0.32)
  the two profiles are of different devices: /device:TPU:1 before, /device:TPU:62 now
where the time goes in v1:
time: 107 us
  Pallas kernels  103 us (96%)
  local copies, waits for them, and re-layouts  3.35 us (3%)
    pallas_call x1, Pallas kernels, local(): pl.pallas_call(kernel, name='mixer_and_attention', out_shape=jax.ShapeDty...  103 us
    unnamed x2, local copies, waits for them, and re-layouts  3.35 us

profile of v1, /device:TPU:62, one launch (start us, length us, event | category | flops | bytes accessed | tf_op | source)
XLA Modules:
  0.0 106.6 jit_solution(8566288520623411661)
XLA Ops:
  0.0 1.5 %copy.12.pattern = s32[2,128,18]{2,1,0:T(8,128)} copy(s32[2,128,18]{1,0,2:T(2,128)} %param.21) | data formatting | bytes 36864 | tf_op args[10]
  1.5 103.3 %mixer_and_attention.1 = bf16[256,1024]{1,0:T(8,128)(2,1)} custom-call(s32[2,128,18]{2,1,0:T(8,128)} %copy.12.pattern, f32[1,1024]{1,0:T(1,128)} %bitcast.3, f32[1,2048]{1,0:T(1,128)} %bitcast.2, bf16[256,2048]{1,0:T(8,128)(2,1)} %hidden_hbm.1, bf16[256,1024]{1,0:T(8,128)(2,1)} %lq_hbm.1, bf16[256,256]{1,0:T(8,128)(2,1)} %lk_hbm.1, bf16[256,256]{1,0:T(8,128)(2,1)} %lv_hbm.1, ...), custom_call_target="tpu_custom_call" | custom-call | tf_op jit(solution)/shard_map/mixer_and_attention/pallas_call | solution.py:441
  104.8 1.9 %copy.14 = bf16[256,1024]{1,0:T(8,128)(2,1)} copy(bf16[256,1024]{1,0:T(8,128)(2,1)} %mixer_and_attention.1) | data formatting | bytes 1048576

commit v2 on v1

v2 whole, which is shorter than its diff:
```python
import heapq
import math

import jax
import jax.numpy as jnp
from jax import lax
from jax.experimental import pallas as pl
from jax.experimental.pallas import tpu as pltpu
from jax.sharding import PartitionSpec as P

HEAD_DIM = 128
HEADS = 8
KV_HEADS = 2
PER_GROUP = HEADS // KV_HEADS
BLOCK = 128
SEL = 18
TOK = 256
D = 2048
NX, NZ = 4, 8
CHIP_TOK = 2 * TOK
PAIRS = SEL // 2
EPSILON = 1e-06
NEG = -1e30
COEF = HEAD_DIM ** (-0.5) * math.log2(math.e)
F32, BF16 = jnp.float32, jnp.bfloat16
MESH = pl.DeviceIdType.MESH

ROWS_A = 208
ROWS_B = CHIP_TOK - ROWS_A
ORDER = [(0, 0), (0, 1), (1, 1), (0, 2), (1, 2), (0, 3), (1, 3), (0, 4)]
STEPS = (4, 3)


def plan():
    ready, free, events, arrived, order = {"x": [], "z": []}, {"x": 0.0, "z": 0.0}, [], {}, []

    def add(copy, needs):
        kind, tensor = copy[:2]
        rank = (tensor, ("a1", "b1", "b2", "a2").index(kind), copy[3:] + copy[2:3] if kind in ("b1", "a2") else copy[2:])
        heapq.heappush(ready["x" if kind in ("a1", "b2") else "z"], (rank, copy, needs))

    def react(copy):
        kind, tensor, rest = copy[0], copy[1], copy[2:]
        if kind == "a1":
            add(("a2", tensor, 0, 1, rest[0]), copy)
            add(("a2", tensor, 1, 1, rest[0]), copy)
        elif kind == "b1":
            direction, step = rest
            if step < STEPS[direction]:
                add(("b1", tensor, direction, step + 1), copy)
            add(("b2", tensor, ORDER.index(rest), 0), copy)
            add(("b2", tensor, ORDER.index(rest), 1), copy)
        elif kind == "b2":
            if rest[1] == rest[0] % 2:
                add(("b2", tensor, rest[0], 2), copy)
        elif rest[1] < STEPS[rest[0]]:
            add(("a2", tensor, rest[0], rest[1] + 1, rest[2]), copy)

    for tensor in range(2):
        for i in (1, 3, 2):
            add(("a1", tensor, i), None)
        for i in range(2):
            add(("b1", tensor, i, 1), None)
            add(("b2", tensor, 0, i), None)
            add(("a2", tensor, i, 1, 0), None)
    now, count = 0.0, 0
    while True:
        for link in "xz":
            if free[link] <= now and ready[link]:
                _, copy, needs = heapq.heappop(ready[link])
                order.append((now, copy, needs, True))
                rows = (ROWS_A if copy[0] in ("a1", "a2") else ROWS_B) * (2 if copy[0] == "a1" and copy[2] == 2 else 1)
                free[link] = now + rows * 256 / 95e3
                arrived[copy] = free[link] + 4.0
                order.append((arrived[copy], copy, copy, False))
                for event in ((arrived[copy], count, copy), (free[link], count + 1, None)):
                    heapq.heappush(events, event)
                count += 2
        if not events:
            return [step[1:] for step in sorted(order, key=lambda step: step[0])]
        now, _, copy = heapq.heappop(events)
        if copy:
            react(copy)


def dot(a, b):
    return jnp.dot(a, b, preferred_element_type=F32)


def dot_nt(a, b):
    return lax.dot_general(a, b, (((1,), (1,)), ((), ())), preferred_element_type=F32)


def dot_tn(a, b):
    return lax.dot_general(a, b, (((0,), (0,)), ((), ())), preferred_element_type=F32)


def kernel(
    pattern_t, lin_gain, soft_gain, hidden_hbm, lq_hbm, lk_hbm, lv_hbm, wo_hbm, wq_hbm, wk_hbm, wv_hbm,
    o_ref,
    hidden, lq, lk, lv, wo, wq, wkv, st_send, st_recv, tot_send, tot_recv, pre_send, pre_recv,
    block0, lin_scores, normed, resid, layer_in, kv_send, q_send, q_all, key_table, value_table, scores, probs, top, norms, bias,
    o_send, o_all,
    load_sem, st_ssem, st_rsem, tot_ssem, tot_rsem, pre_ssem, pre_rsem, sib_ssem, sib_rsem,
    a1_ssem, a1_rsem, a2_ssem, a2_rsem, b1_ssem, b1_rsem, b2_ssem, b2_rsem,
):
    me = lax.axis_index("seq")
    core = lax.rem(me, 2)
    chip = me // 2
    z = lax.rem(chip, NZ)
    x = chip // NZ
    sign = 1 - 2 * core
    row_pos = z * 2 + core

    def dev(cx, cz, cc):
        return {"seq": (lax.rem(cx + 2 * NX, NX) * NZ + lax.rem(cz + 2 * NZ, NZ)) * 2 + cc}

    sibling = dev(x, z, 1 - core)

    def remote(src, dst, ssem, rsem, device):
        return pltpu.make_async_remote_copy(
            src_ref=src, dst_ref=dst, send_sem=ssem, recv_sem=rsem, device_id=device, device_id_type=MESH
        )

    barrier = pltpu.get_barrier_semaphore()
    for i in range(1, 2 * NZ):
        pos = lax.rem(row_pos + i, 2 * NZ)
        pl.semaphore_signal(barrier, inc=1, device_id={"seq": x * 2 * NZ + pos}, device_id_type=MESH)
    for i in range(1, NX):
        pl.semaphore_signal(barrier, inc=1, device_id=dev(x + i, z, core), device_id_type=MESH)

    own_q = pl.ds(pl.multiple_of(core * 512, 512), 512)
    sib_q = pl.ds(pl.multiple_of((1 - core) * 512, 512), 512)
    own_h = pl.ds(pl.multiple_of(core * 128, 128), 128)
    sib_h = pl.ds(pl.multiple_of((1 - core) * 128, 128), 128)
    loads = [
        (lk_hbm, lk),
        (lv_hbm, lv),
        (lq_hbm, lq),
        (wo_hbm, wo),
        (hidden_hbm, hidden),
        (wk_hbm.at[:, own_h], wkv.at[0, :, 0:128]),
        (wv_hbm.at[:, own_h], wkv.at[0, :, 128:256]),
        (wk_hbm.at[:, sib_h], wkv.at[1, :, 0:128]),
        (wv_hbm.at[:, sib_h], wkv.at[1, :, 128:256]),
        (wq_hbm.at[:, own_q], wq.at[0]),
        (wq_hbm.at[:, sib_q], wq.at[1]),
    ]
    loads = [pltpu.make_async_copy(src, dst, load_sem.at[i]) for i, (src, dst) in enumerate(loads)]
    for copy in loads[:3]:
        copy.start()
    loads[0].wait()
    loads[1].wait()

    for g in range(KV_HEADS):
        cols = slice(g * 128, g * 128 + 128)
        first = dot_tn(lk[0:128, cols], lv[0:128, cols])
        second = dot_tn(lk[128:256, cols], lv[128:256, cols])
        block0[g] = first.astype(BF16)
        st_send[g] = (first + second).astype(BF16).reshape(NZ, 16, 128)

    pl.semaphore_wait(barrier, 2 * NZ - 1 + NX - 1)

    st_copies = []
    for i in range(1, 2 * NZ):
        pos = lax.rem(row_pos + i, 2 * NZ)
        copy = remote(
            st_send.at[lax.rem(pos, 2), pos // 2], st_recv.at[row_pos], st_ssem.at[i - 1], st_rsem.at[i - 1],
            {"seq": x * 2 * NZ + pos},
        )
        copy.start()
        st_copies.append(copy)
    for copy in loads[3:]:
        copy.start()
    st_recv[row_pos] = st_send[core, z]

    loads[2].wait()
    tri = lax.broadcasted_iota(jnp.int32, (128, 128), 0) >= lax.broadcasted_iota(jnp.int32, (128, 128), 1)
    tri4 = jnp.concatenate([tri] * PER_GROUP, axis=0)

    def stacked(n, g):
        return jnp.concatenate(
            [lq[n * 128 : n * 128 + 128, (g * PER_GROUP + h) * 128 : (g * PER_GROUP + h) * 128 + 128] for h in range(PER_GROUP)],
            axis=0,
        )

    for n in range(2):
        for g in range(KV_HEADS):
            keys = lk[n * 128 : n * 128 + 128, g * 128 : g * 128 + 128]
            lin_scores[n, g] = jnp.where(tri4, dot_nt(stacked(n, g), keys), 0.0).astype(BF16)

    for copy in st_copies:
        copy.wait()
    total = st_recv[0].astype(F32)
    for i in range(1, 2 * NZ):
        total = total + st_recv[i].astype(F32)
    tot_send[...] = total
    tot_copies = []
    for i in range(1, NX):
        copy = remote(tot_send, tot_recv.at[i - 1], tot_ssem.at[i - 1], tot_rsem.at[i - 1], dev(x + i, z, core))
        copy.start()
        tot_copies.append(copy)
    for copy in tot_copies:
        copy.wait()
    running = jnp.zeros((16, 128), F32)
    for i in range(1, NX):
        running = running + jnp.where(x - i >= 0, tot_recv[i - 1], 0.0)
    for i in range(2 * NZ):
        pre_send[i] = running.astype(BF16)
        running = running + st_recv[i].astype(F32)
    pre_copies = []
    for i in range(1, 2 * NZ):
        pos = lax.rem(row_pos + i, 2 * NZ)
        copy = remote(
            pre_send.at[pos], pre_recv.at[core, z], pre_ssem.at[i - 1], pre_rsem.at[i - 1], {"seq": x * 2 * NZ + pos}
        )
        copy.start()
        pre_copies.append(copy)
    pre_recv[core, z] = pre_send[row_pos]
    for copy in pre_copies:
        copy.wait()

    for n in range(2):
        for g in range(KV_HEADS):
            state = pre_recv[g].reshape(128, 128)
            values = lv[n * 128 : n * 128 + 128, g * 128 : g * 128 + 128]
            if n == 0:
                mix = dot(
                    jnp.concatenate([stacked(n, g), lin_scores[n, g]], axis=1), jnp.concatenate([state, values], axis=0)
                )
            else:
                qs = stacked(n, g)
                mix = dot(
                    jnp.concatenate([qs, qs, lin_scores[n, g]], axis=1),
                    jnp.concatenate([state, block0[g], values], axis=0),
                )
            mix = mix * lax.rsqrt(jnp.mean(mix * mix, axis=-1, keepdims=True) + EPSILON)
            for h in range(PER_GROUP):
                cols = slice((g * PER_GROUP + h) * 128, (g * PER_GROUP + h) * 128 + 128)
                normed[n * 128 : n * 128 + 128, cols] = (mix[h * 128 : h * 128 + 128] * lin_gain[:, cols]).astype(BF16)

    loads[3].wait()
    loads[4].wait()
    squares = jnp.zeros((TOK, 128), F32)
    for t in range(4):
        cols = slice(t * 512, t * 512 + 512)
        res = (hidden[:, cols].astype(F32) + dot(normed[...], wo[:, cols])).astype(BF16)
        resid[:, cols] = res
        wide = res.astype(F32)
        wide = wide * wide
        for s in range(4):
            squares = squares + wide[:, s * 128 : s * 128 + 128]
    factor = lax.rsqrt(jnp.sum(squares, axis=-1, keepdims=True) * (1.0 / D) + EPSILON)
    for t in range(4):
        cols = slice(t * 512, t * 512 + 512)
        layer_in[:, cols] = (resid[:, cols].astype(F32) * factor * soft_gain[:, cols]).astype(BF16)

    for i in range(5, 9):
        loads[i].wait()
    tables = [t.reshape(NX * NZ * CHIP_TOK, 128) for t in (key_table, value_table)]
    my_rows = pl.ds(pl.multiple_of(me * TOK, TOK), TOK)
    sib_copies = []
    for tensor in range(2):
        kv_send[tensor] = dot(layer_in[...], wkv[1, :, tensor * 128 : tensor * 128 + 128]).astype(BF16)
        copy = remote(kv_send.at[tensor], tables[tensor].at[my_rows], sib_ssem.at[tensor], sib_rsem.at[tensor], sibling)
        copy.start()
        sib_copies.append(copy)
    for tensor in range(2):
        tables[tensor][my_rows] = dot(layer_in[...], wkv[0, :, tensor * 128 : tensor * 128 + 128]).astype(BF16)
    for copy in sib_copies:
        copy.wait()

    started, landed = {}, set()
    sems = {"a1": (a1_ssem, a1_rsem), "a2": (a2_ssem, a2_rsem), "b1": (b1_ssem, b1_rsem), "b2": (b2_ssem, b2_rsem)}

    def launch(copy):
        kind, tensor, rest = copy[0], copy[1], copy[2:]

        def hop(direction, distance):
            return (-sign if direction == 0 else sign) * distance

        sx, sz = x, z
        if kind == "a1":
            index, to = (rest[0] - 1,), dev(x + rest[0], z, core)
        elif kind == "b1":
            sz, index = z + hop(rest[0], rest[1] - 1), (rest[0], rest[1] - 1)
            to = dev(x, z - hop(rest[0], 1), core)
        elif kind == "a2":
            sx, sz, index = x - rest[2], z + hop(rest[0], rest[1] - 1), (rest[0], rest[1] - 1, rest[2])
            to = dev(x, z - hop(rest[0], 1), core)
        else:
            r, j = rest
            sz, index = z + hop(*ORDER[r]), (r, j)
            along = (sign, -sign)[j if j < 2 else r % 2]
            if j == 2:
                sx = x - along
            to = dev(x + along, z, core)
        first, count = (0, ROWS_A) if kind in ("a1", "a2") else (ROWS_A, ROWS_B)
        src = lax.rem(sx + 2 * NX, NX) * NZ + lax.rem(sz + 2 * NZ, NZ)
        part = tables[tensor].at[pl.ds(pl.multiple_of(src * CHIP_TOK + first, 16), count)]
        ssem, rsem = sems[kind]
        started[copy] = remote(part, part, ssem.at[(tensor, *index)], rsem.at[(tensor, *index)], to)
        started[copy].start()

    def land(copy):
        if copy not in landed:
            landed.add(copy)
            started[copy].wait_recv()

    order = plan()
    missing = {copy for copy, _, _ in order if copy[1] == 0}
    first_wait = next(i for i, (_, needs, _) in enumerate(order) if needs is not None)
    for copy, _, _ in order[:first_wait]:
        launch(copy)

    loads[9].wait()
    loads[10].wait()

    def put_queries(part, write):
        q = dot(layer_in[...], wq[part]).astype(BF16)
        for n in range(2):
            for h in range(PER_GROUP):
                write(n, h, q[n * 128 : n * 128 + 128, h * 128 : h * 128 + 128])

    def write_send(n, h, value):
        q_send[n, h * 128 : h * 128 + 128, :] = value

    def write_own(n, h, value):
        q_all[core * 2 + n, h * 128 : h * 128 + 128, :] = value

    put_queries(1, write_send)
    q_copy = remote(q_send, q_all.at[pl.ds(core * 2, 2)], sib_ssem.at[2], sib_rsem.at[2], sibling)
    q_copy.start()
    put_queries(0, write_own)

    def find_repeats(i, carry):
        entries = [pattern_t[j, core, chip * 4 + i] for j in range(SEL)]
        for j in range(SEL):
            value = jnp.float32(0.0)
            for e in range(j):
                value = jnp.where(entries[e] == entries[j], jnp.float32(NEG), value)
            bias[i, j] = value
        return carry

    lax.fori_loop(0, 4, find_repeats, 0)

    def block_of(i, j):
        return pattern_t[j, core, chip * 4 + i]

    def score(i, pairs):
        q = q_all[i]
        best = None if pairs[0] == 0 else top[...]
        for p in pairs:
            keys = jnp.concatenate([key_table[block_of(i, 2 * p)], key_table[block_of(i, 2 * p + 1)]], axis=0)
            s = dot_nt(q, keys) * COEF
            left, right = s[:, 0:128] + bias[i, 2 * p], s[:, 128:256] + bias[i, 2 * p + 1]
            if p == 0:
                left = jnp.where(tri4, left, NEG)
            scores[p, :, 0:128] = left
            scores[p, :, 128:256] = right
            both = jnp.maximum(left, right)
            best = both if best is None else jnp.maximum(best, both)
        if pairs[-1] == PAIRS - 1:
            best = jnp.broadcast_to(jnp.max(best, axis=-1, keepdims=True), (512, 128))
        top[...] = best

    def weigh(i, pairs):
        total = None if pairs[0] == 0 else norms[i]
        for p in pairs:
            left = jnp.exp2(scores[p, :, 0:128] - top[...])
            right = jnp.exp2(scores[p, :, 128:256] - top[...])
            probs[i, :, p * 256 : p * 256 + 128] = left.astype(BF16)
            probs[i, :, p * 256 + 128 : p * 256 + 256] = right.astype(BF16)
            total = left + right if total is None else total + (left + right)
        if pairs[-1] == PAIRS - 1:
            total = jnp.broadcast_to(1.0 / jnp.sum(total, axis=-1, keepdims=True), (512, 128))
        norms[i] = total

    thirds = [range(0, 3), range(3, 6), range(6, 9)]
    work = [(f, i, pairs) for i in range(4) for f in (score, weigh) for pairs in thirds]
    work.reverse()

    for copy, needs, starts in order[first_wait:]:
        if needs is not None:
            land(needs)
            missing.discard(needs)
        if starts:
            launch(copy)
        if not missing and work:
            if len(work) == 24:
                q_copy.wait()
            part, i, pairs = work.pop()
            part(i, pairs)
    for copy in started.values():
        copy.wait_send()

    def attend(part, n):
        i = (1 - core if part == 0 else core) * 2 + n
        values = jnp.concatenate([value_table[block_of(i, j)] for j in range(SEL)], axis=0)
        out = dot(probs[i], values)
        rows = pl.ds(pl.multiple_of(n * 128, 128), 128)
        for h in range(PER_GROUP):
            value = (out[h * 128 : h * 128 + 128] * norms[i, h * 128 : h * 128 + 128, :]).astype(BF16)
            if part == 0:
                o_send[rows, h * 128 : h * 128 + 128] = value
            else:
                o_all[core, rows, h * 128 : h * 128 + 128] = value

    @pl.loop(0, 2)
    def _(n):
        attend(0, n)

    o_copy = remote(o_send, o_all.at[core], sib_ssem.at[3], sib_rsem.at[3], sibling)
    o_copy.start()

    @pl.loop(0, 2)
    def _(n):
        attend(1, n)

    o_copy.wait()
    o_ref[:, 0:512] = o_all[0]
    o_ref[:, 512:1024] = o_all[1]


def local(hidden_in, lin_query, lin_key, lin_value, lin_gain, lin_out_weight, soft_gain, soft_wq, soft_wk, soft_wv, pattern):
    dma = pltpu.SemaphoreType.DMA
    vmem, anywhere = pl.BlockSpec(memory_space=pltpu.VMEM), pl.BlockSpec(memory_space=pl.ANY)
    scratch = [
        pltpu.VMEM((TOK, D), BF16),
        pltpu.VMEM((TOK, 1024), BF16),
        pltpu.VMEM((TOK, 256), BF16),
        pltpu.VMEM((TOK, 256), BF16),
        pltpu.VMEM((1024, D), BF16),
        pltpu.VMEM((2, D, 512), BF16),
        pltpu.VMEM((2, D, 256), BF16),
        pltpu.VMEM((2, NZ, 16, 128), BF16),
        pltpu.VMEM((2 * NZ, 16, 128), BF16),
        pltpu.VMEM((16, 128), F32),
        pltpu.VMEM((NX - 1, 16, 128), F32),
        pltpu.VMEM((2 * NZ, 16, 128), BF16),
        pltpu.VMEM((2, NZ, 16, 128), BF16),
        pltpu.VMEM((2, 128, 128), BF16),
        pltpu.VMEM((2, 2, 512, 128), BF16),
        pltpu.VMEM((TOK, 1024), BF16),
        pltpu.VMEM((TOK, D), BF16),
        pltpu.VMEM((TOK, D), BF16),
        pltpu.VMEM((2, TOK, 128), BF16),
        pltpu.VMEM((2, 512, 128), BF16),
        pltpu.VMEM((4, 512, 128), BF16),
        pltpu.VMEM((NX * NZ * CHIP_TOK // BLOCK, BLOCK, 128), BF16),
        pltpu.VMEM((NX * NZ * CHIP_TOK // BLOCK, BLOCK, 128), BF16),
        pltpu.VMEM((PAIRS, 512, 256), F32),
        pltpu.VMEM((4, 512, SEL * BLOCK), BF16),
        pltpu.VMEM((512, 128), F32),
        pltpu.VMEM((4, 512, 128), F32),
        pltpu.SMEM((4, SEL), F32),
        pltpu.VMEM((TOK, 512), BF16),
        pltpu.VMEM((2, TOK, 512), BF16),
        dma((11,)),
        dma((2 * NZ - 1,)), dma((2 * NZ - 1,)),
        dma((NX - 1,)), dma((NX - 1,)),
        dma((2 * NZ - 1,)), dma((2 * NZ - 1,)),
        dma((4,)), dma((4,)),
        dma((2, NX - 1)), dma((2, NX - 1)),
        dma((2, 2, 4, NX)), dma((2, 2, 4, NX)),
        dma((2, 2, 4)), dma((2, 2, 4)),
        dma((2, NZ, 3)), dma((2, NZ, 3)),
    ]
    return pl.pallas_call(
        kernel,
        name="mixer_and_attention",
        out_shape=jax.ShapeDtypeStruct((TOK, 1024), BF16),
        in_specs=[pl.BlockSpec(memory_space=pltpu.SMEM), vmem, vmem] + [anywhere] * 8,
        out_specs=vmem,
        scratch_shapes=scratch,
        compiler_params=pltpu.CompilerParams(collective_id=0, has_side_effects=True, vmem_limit_bytes=56 << 20),
    )(
        pattern.transpose(2, 0, 1), lin_gain.reshape(1, 1024), soft_gain.reshape(1, D),
        hidden_in, lin_query, lin_key, lin_value, lin_out_weight, soft_wq, soft_wk, soft_wv,
    )


def solution(mesh):
    whole, split = P(), P(("dp", "seq"), None)
    in_specs = (split, split, split, split) + (whole,) * 7
    return jax.shard_map(local, mesh=mesh, in_specs=in_specs, out_specs=split, check_vma=False)
```

time: 107 us -> 88.4 us (0.83)
  the two profiles are of different devices: /device:TPU:62 before, /device:TPU:1 now
where the time goes in v2:
time: 88.4 us; the launch traced here: 88.2 us
  Pallas kernels  86.3 us (98%)
  local copies, waits for them, and re-layouts  1.87 us (2%)
    pallas_call x1, Pallas kernels, local(): pl.pallas_call(kernel, name='mixer_and_attention', out_shape=jax.ShapeDty...  86.3 us
    unnamed x1, local copies, waits for them, and re-layouts  1.87 us

profile of v2, /device:TPU:1, one launch (start us, length us, event | category | flops | bytes accessed | tf_op | source)
XLA Modules:
  0.0 88.2 jit_solution(5525262941347753086)
XLA Ops:
  0.0 86.3 %mixer_and_attention.1 = bf16[256,1024]{1,0:T(8,128)(2,1)} custom-call(s32[18,2,128]{2,1,0:T(2,128)} %bitcast.3, f32[1,1024]{1,0:T(1,128)} %bitcast.5, f32[1,2048]{1,0:T(1,128)} %bitcast.4, bf16[256,2048]{1,0:T(8,128)(2,1)} %hidden_hbm.1, bf16[256,1024]{1,0:T(8,128)(2,1)} %lq_hbm.1, bf16[256,256]{1,0:T(8,128)(2,1)} %lk_hbm.1, bf16[256,256]{1,0:T(8,128)(2,1)} %lv_hbm.1, ...), custom_call_target="tpu_custom_call" | custom-call | tf_op jit(solution)/shard_map/mixer_and_attention/pallas_call | solution.py:469
  86.3 1.9 %copy.13 = bf16[256,1024]{1,0:T(8,128)(2,1)} copy(bf16[256,1024]{1,0:T(8,128)(2,1)} %mixer_and_attention.1) | data formatting | bytes 1048576

commit v3 on v2

--- a/solution.py
+++ b/solution.py
@@ -27,8 +27,10 @@
 
 ROWS_A = 208
 ROWS_B = CHIP_TOK - ROWS_A
+FAR_FIRST = sorted(range(1, 2 * NZ), key=lambda i: -min(i, 2 * NZ - i))
 ORDER = [(0, 0), (0, 1), (1, 1), (0, 2), (1, 2), (0, 3), (1, 3), (0, 4)]
 STEPS = (4, 3)
+LINK, LATENCY_US, SIBLING_US = 95000.0, 5.0, 3.0
 
 
 def plan():
@@ -41,7 +43,11 @@
 
     def react(copy):
         kind, tensor, rest = copy[0], copy[1], copy[2:]
-        if kind == "a1":
+        if kind == "sib":
+            for i in range(2):
+                add(("b1", tensor, i, 1), copy)
+                add(("b2", tensor, 0, i), copy)
+        elif kind == "a1":
             add(("a2", tensor, 0, 1, rest[0]), copy)
             add(("a2", tensor, 1, 1, rest[0]), copy)
         elif kind == "b1":
@@ -60,18 +66,17 @@
         for i in (1, 3, 2):
             add(("a1", tensor, i), None)
         for i in range(2):
-            add(("b1", tensor, i, 1), None)
-            add(("b2", tensor, 0, i), None)
             add(("a2", tensor, i, 1, 0), None)
-    now, count = 0.0, 0
+        heapq.heappush(events, (SIBLING_US + 0.5 * tensor, tensor, ("sib", tensor)))
+    now, count = 0.0, 2
     while True:
         for link in "xz":
             if free[link] <= now and ready[link]:
                 _, copy, needs = heapq.heappop(ready[link])
                 order.append((now, copy, needs, True))
                 rows = (ROWS_A if copy[0] in ("a1", "a2") else ROWS_B) * (2 if copy[0] == "a1" and copy[2] == 2 else 1)
-                free[link] = now + rows * 256 / 95e3
-                arrived[copy] = free[link] + 4.0
+                free[link] = now + rows * 256 / LINK
+                arrived[copy] = free[link] + LATENCY_US
                 order.append((arrived[copy], copy, copy, False))
                 for event in ((arrived[copy], count, copy), (free[link], count + 1, None)):
                     heapq.heappush(events, event)
@@ -121,13 +126,6 @@
         return pltpu.make_async_remote_copy(
             src_ref=src, dst_ref=dst, send_sem=ssem, recv_sem=rsem, device_id=device, device_id_type=MESH
         )
-
-    barrier = pltpu.get_barrier_semaphore()
-    for i in range(1, 2 * NZ):
-        pos = lax.rem(row_pos + i, 2 * NZ)
-        pl.semaphore_signal(barrier, inc=1, device_id={"seq": x * 2 * NZ + pos}, device_id_type=MESH)
-    for i in range(1, NX):
-        pl.semaphore_signal(barrier, inc=1, device_id=dev(x + i, z, core), device_id_type=MESH)
 
     own_q = pl.ds(pl.multiple_of(core * 512, 512), 512)
     sib_q = pl.ds(pl.multiple_of((1 - core) * 512, 512), 512)
@@ -149,6 +147,14 @@
     loads = [pltpu.make_async_copy(src, dst, load_sem.at[i]) for i, (src, dst) in enumerate(loads)]
     for copy in loads[:3]:
         copy.start()
+
+    barrier = pltpu.get_barrier_semaphore()
+    for i in FAR_FIRST:
+        pos = lax.rem(row_pos + i, 2 * NZ)
+        pl.semaphore_signal(barrier, inc=1, device_id={"seq": x * 2 * NZ + pos}, device_id_type=MESH)
+    for i in range(1, NX):
+        pl.semaphore_signal(barrier, inc=1, device_id=dev(x + i, z, core), device_id_type=MESH)
+
     loads[0].wait()
     loads[1].wait()
 
@@ -162,7 +168,7 @@
     pl.semaphore_wait(barrier, 2 * NZ - 1 + NX - 1)
 
     st_copies = []
-    for i in range(1, 2 * NZ):
+    for i in FAR_FIRST:
         pos = lax.rem(row_pos + i, 2 * NZ)
         copy = remote(
             st_send.at[lax.rem(pos, 2), pos // 2], st_recv.at[row_pos], st_ssem.at[i - 1], st_rsem.at[i - 1],
@@ -190,7 +196,7 @@
             lin_scores[n, g] = jnp.where(tri4, dot_nt(stacked(n, g), keys), 0.0).astype(BF16)
 
     for copy in st_copies:
-        copy.wait()
+        copy.wait_recv()
     total = st_recv[0].astype(F32)
     for i in range(1, 2 * NZ):
         total = total + st_recv[i].astype(F32)
@@ -201,7 +207,7 @@
         copy.start()
         tot_copies.append(copy)
     for copy in tot_copies:
-        copy.wait()
+        copy.wait_recv()
     running = jnp.zeros((16, 128), F32)
     for i in range(1, NX):
         running = running + jnp.where(x - i >= 0, tot_recv[i - 1], 0.0)
@@ -209,7 +215,7 @@
         pre_send[i] = running.astype(BF16)
         running = running + st_recv[i].astype(F32)
     pre_copies = []
-    for i in range(1, 2 * NZ):
+    for i in FAR_FIRST:
         pos = lax.rem(row_pos + i, 2 * NZ)
         copy = remote(
             pre_send.at[pos], pre_recv.at[core, z], pre_ssem.at[i - 1], pre_rsem.at[i - 1], {"seq": x * 2 * NZ + pos}
@@ -218,7 +224,7 @@
         pre_copies.append(copy)
     pre_recv[core, z] = pre_send[row_pos]
     for copy in pre_copies:
-        copy.wait()
+        copy.wait_recv()
 
     for n in range(2):
         for g in range(KV_HEADS):
@@ -260,15 +266,15 @@
     tables = [t.reshape(NX * NZ * CHIP_TOK, 128) for t in (key_table, value_table)]
     my_rows = pl.ds(pl.multiple_of(me * TOK, TOK), TOK)
     sib_copies = []
+    both = dot(layer_in[...], wkv[1]).astype(BF16)
     for tensor in range(2):
-        kv_send[tensor] = dot(layer_in[...], wkv[1, :, tensor * 128 : tensor * 128 + 128]).astype(BF16)
+        kv_send[tensor] = both[:, tensor * 128 : tensor * 128 + 128]
         copy = remote(kv_send.at[tensor], tables[tensor].at[my_rows], sib_ssem.at[tensor], sib_rsem.at[tensor], sibling)
         copy.start()
         sib_copies.append(copy)
+    both = dot(layer_in[...], wkv[0]).astype(BF16)
     for tensor in range(2):
-        tables[tensor][my_rows] = dot(layer_in[...], wkv[0, :, tensor * 128 : tensor * 128 + 128]).astype(BF16)
-    for copy in sib_copies:
-        copy.wait()
+        tables[tensor][my_rows] = both[:, tensor * 128 : tensor * 128 + 128]
 
     started, landed = {}, set()
     sems = {"a1": (a1_ssem, a1_rsem), "a2": (a2_ssem, a2_rsem), "b1": (b1_ssem, b1_rsem), "b2": (b2_ssem, b2_rsem)}
@@ -295,7 +301,10 @@
             if j == 2:
                 sx = x - along
             to = dev(x + along, z, core)
-        first, count = (0, ROWS_A) if kind in ("a1", "a2") else (ROWS_A, ROWS_B)
+        if kind in ("a1", "a2"):
+            first, count = core * ROWS_B, ROWS_A
+        else:
+            first, count = (1 - core) * ROWS_A, ROWS_B
         src = lax.rem(sx + 2 * NX, NX) * NZ + lax.rem(sz + 2 * NZ, NZ)
         part = tables[tensor].at[pl.ds(pl.multiple_of(src * CHIP_TOK + first, 16), count)]
         ssem, rsem = sems[kind]
@@ -305,14 +314,10 @@
     def land(copy):
         if copy not in landed:
             landed.add(copy)
-            started[copy].wait_recv()
+            (sib_copies[copy[1]] if copy[0] == "sib" else started[copy]).wait_recv()
 
     order = plan()
     missing = {copy for copy, _, _ in order if copy[1] == 0}
-    first_wait = next(i for i, (_, needs, _) in enumerate(order) if needs is not None)
-    for copy, _, _ in order[:first_wait]:
-        launch(copy)
-
     loads[9].wait()
     loads[10].wait()
 
@@ -328,21 +333,7 @@
     def write_own(n, h, value):
         q_all[core * 2 + n, h * 128 : h * 128 + 128, :] = value
 
-    put_queries(1, write_send)
     q_copy = remote(q_send, q_all.at[pl.ds(core * 2, 2)], sib_ssem.at[2], sib_rsem.at[2], sibling)
-    q_copy.start()
-    put_queries(0, write_own)
-
-    def find_repeats(i, carry):
-        entries = [pattern_t[j, core, chip * 4 + i] for j in range(SEL)]
-        for j in range(SEL):
-            value = jnp.float32(0.0)
-            for e in range(j):
-                value = jnp.where(entries[e] == entries[j], jnp.float32(NEG), value)
-            bias[i, j] = value
-        return carry
-
-    lax.fori_loop(0, 4, find_repeats, 0)
 
     def block_of(i, j):
         return pattern_t[j, core, chip * 4 + i]
@@ -380,8 +371,27 @@
     work = [(f, i, pairs) for i in range(4) for f in (score, weigh) for pairs in thirds]
     work.reverse()
 
-    for copy, needs, starts in order[first_wait:]:
+    def find_repeats(i, carry):
+        entries = [pattern_t[j, core, chip * 4 + i] for j in range(SEL)]
+        for j in range(SEL):
+            value = jnp.float32(0.0)
+            for e in range(j):
+                value = jnp.where(entries[e] == entries[j], jnp.float32(NEG), value)
+            bias[i, j] = value
+        return carry
+
+
+    waits = 0
+    for copy, needs, starts in order:
         if needs is not None:
+            if needs not in landed and waits == 0:
+                put_queries(1, write_send)
+                q_copy.start()
+                waits = 1
+            elif needs not in landed and waits == 1 and needs[0] != "sib":
+                put_queries(0, write_own)
+                lax.fori_loop(0, 4, find_repeats, 0)
+                waits = 2
             land(needs)
             missing.discard(needs)
         if starts:
@@ -391,8 +401,9 @@
                 q_copy.wait()
             part, i, pairs = work.pop()
             part(i, pairs)
-    for copy in started.values():
-        copy.wait_send()
+    while work:
+        part, i, pairs = work.pop()
+        part(i, pairs)
 
     def attend(part, n):
         i = (1 - core if part == 0 else core) * 2 + n
@@ -417,6 +428,8 @@
     def _(n):
         attend(1, n)
 
+    for copy in [*st_copies, *tot_copies, *pre_copies, *sib_copies, *started.values()]:
+        copy.wait_send()
     o_copy.wait()
     o_ref[:, 0:512] = o_all[0]
     o_ref[:, 512:1024] = o_all[1]

time: 88.4 us -> 85.8 us (0.971)
  Pallas kernels: 86.3 us -> 83.8 us
    pallas_call x1, Pallas kernels: 86.3 us -> 83.8 us  [local(): pl.pallas_call(kernel, name='mixer_and_attention', out_shape=jax.ShapeDty...]
where the time goes in v3:
time: 85.8 us; the launch traced here: 85.6 us
  Pallas kernels  83.8 us (98%)
  local copies, waits for them, and re-layouts  1.87 us (2%)
    pallas_call x1, Pallas kernels, local(): pl.pallas_call(kernel, name='mixer_and_attention', out_shape=jax.ShapeDty...  83.8 us
    unnamed x1, local copies, waits for them, and re-layouts  1.87 us

profile of v3, /device:TPU:1, one launch (start us, length us, event | category | flops | bytes accessed | tf_op | source)
XLA Modules:
  0.0 85.6 jit_solution(196670950333445466)
XLA Ops:
  0.0 83.8 %mixer_and_attention.1 = bf16[256,1024]{1,0:T(8,128)(2,1)} custom-call(s32[18,2,128]{2,1,0:T(2,128)} %bitcast.3, f32[1,1024]{1,0:T(1,128)} %bitcast.5, f32[1,2048]{1,0:T(1,128)} %bitcast.4, bf16[256,2048]{1,0:T(8,128)(2,1)} %hidden_hbm.1, bf16[256,1024]{1,0:T(8,128)(2,1)} %lq_hbm.1, bf16[256,256]{1,0:T(8,128)(2,1)} %lk_hbm.1, bf16[256,256]{1,0:T(8,128)(2,1)} %lv_hbm.1, ...), custom_call_target="tpu_custom_call" | custom-call | tf_op jit(solution)/shard_map/mixer_and_attention/pallas_call | solution.py:482
  83.8 1.9 %copy.13 = bf16[256,1024]{1,0:T(8,128)(2,1)} copy(bf16[256,1024]{1,0:T(8,128)(2,1)} %mixer_and_attention.1) | data formatting | bytes 1048576

commit v4 on v3

--- a/solution.py
+++ b/solution.py
@@ -101,11 +101,12 @@
 
 
 def kernel(
-    pattern_t, lin_gain, soft_gain, hidden_hbm, lq_hbm, lk_hbm, lv_hbm, wo_hbm, wq_hbm, wk_hbm, wv_hbm,
+    pattern_hbm, lin_gain_hbm, soft_gain_hbm, hidden_hbm, lq_hbm, lk_hbm, lv_hbm, wo_hbm, wq_hbm, wk_hbm, wv_hbm,
     o_ref,
     hidden, lq, lk, lv, wo, wq, wkv, st_send, st_recv, tot_send, tot_recv, pre_send, pre_recv,
     block0, lin_scores, normed, resid, layer_in, kv_send, q_send, q_all, key_table, value_table, scores, probs, top, norms, bias,
     o_send, o_all,
+    pattern_t, lin_gain, soft_gain,
     load_sem, st_ssem, st_rsem, tot_ssem, tot_rsem, pre_ssem, pre_rsem, sib_ssem, sib_rsem,
     a1_ssem, a1_rsem, a2_ssem, a2_rsem, b1_ssem, b1_rsem, b2_ssem, b2_rsem,
 ):
@@ -143,6 +144,9 @@
         (wv_hbm.at[:, sib_h], wkv.at[1, :, 128:256]),
         (wq_hbm.at[:, own_q], wq.at[0]),
         (wq_hbm.at[:, sib_q], wq.at[1]),
+        (lin_gain_hbm, lin_gain),
+        (soft_gain_hbm, soft_gain),
+        (pattern_hbm, pattern_t),
     ]
     loads = [pltpu.make_async_copy(src, dst, load_sem.at[i]) for i, (src, dst) in enumerate(loads)]
     for copy in loads[:3]:
@@ -226,6 +230,9 @@
     for copy in pre_copies:
         copy.wait_recv()
 
+    loads[11].wait()
+    loads[12].wait()
+    loads[13].wait()
     for n in range(2):
         for g in range(KV_HEADS):
             state = pre_recv[g].reshape(128, 128)
@@ -469,7 +476,10 @@
         pltpu.SMEM((4, SEL), F32),
         pltpu.VMEM((TOK, 512), BF16),
         pltpu.VMEM((2, TOK, 512), BF16),
-        dma((11,)),
+        pltpu.SMEM((SEL, KV_HEADS, 128), jnp.int32),
+        pltpu.VMEM((1, 1024), F32),
+        pltpu.VMEM((1, D), F32),
+        dma((14,)),
         dma((2 * NZ - 1,)), dma((2 * NZ - 1,)),
         dma((NX - 1,)), dma((NX - 1,)),
         dma((2 * NZ - 1,)), dma((2 * NZ - 1,)),
@@ -483,7 +493,7 @@
         kernel,
         name="mixer_and_attention",
         out_shape=jax.ShapeDtypeStruct((TOK, 1024), BF16),
-        in_specs=[pl.BlockSpec(memory_space=pltpu.SMEM), vmem, vmem] + [anywhere] * 8,
+        in_specs=[anywhere] * 11,
         out_specs=vmem,
         scratch_shapes=scratch,
         compiler_params=pltpu.CompilerParams(collective_id=0, has_side_effects=True, vmem_limit_bytes=56 << 20),

time: 85.8 us -> 85.1 us (level)
  no operation moved by 1% of the time
where the time goes in v4:
time: 85.1 us; the launch traced here: 85 us
  Pallas kernels  83.1 us (98%)
  local copies, waits for them, and re-layouts  1.87 us (2%)
    pallas_call x1, Pallas kernels, local(): pl.pallas_call(kernel, name='mixer_and_attention', out_shape=jax.ShapeDty...  83.1 us
    unnamed x1, local copies, waits for them, and re-layouts  1.87 us

profile of v4, /device:TPU:1, one launch (start us, length us, event | category | flops | bytes accessed | tf_op | source)
XLA Modules:
  0.0 85.0 jit_solution(301950144060276262)
XLA Ops:
  0.0 83.1 %mixer_and_attention.1 = bf16[256,1024]{1,0:T(8,128)(2,1)} custom-call(s32[18,2,128]{2,1,0:T(2,128)} %bitcast.3, f32[1,1024]{1,0:T(1,128)} %bitcast.5, f32[1,2048]{1,0:T(1,128)} %bitcast.4, bf16[256,2048]{1,0:T(8,128)(2,1)} %hidden_hbm.1, bf16[256,1024]{1,0:T(8,128)(2,1)} %lq_hbm.1, bf16[256,256]{1,0:T(8,128)(2,1)} %lk_hbm.1, bf16[256,256]{1,0:T(8,128)(2,1)} %lv_hbm.1, ...), custom_call_target="tpu_custom_call" | custom-call | tf_op jit(solution)/shard_map/mixer_and_attention/pallas_call | solution.py:492
  83.1 1.9 %copy.13 = bf16[256,1024]{1,0:T(8,128)(2,1)} copy(bf16[256,1024]{1,0:T(8,128)(2,1)} %mixer_and_attention.1) | data formatting | bytes 1048576

commit v5 on v4

--- a/solution.py
+++ b/solution.py
@@ -416,7 +416,7 @@
         i = (1 - core if part == 0 else core) * 2 + n
         values = jnp.concatenate([value_table[block_of(i, j)] for j in range(SEL)], axis=0)
         out = dot(probs[i], values)
-        rows = pl.ds(pl.multiple_of(n * 128, 128), 128)
+        rows = pl.ds(n * 128 if part == 0 else pl.multiple_of(n * 128, 128), 128)
         for h in range(PER_GROUP):
             value = (out[h * 128 : h * 128 + 128] * norms[i, h * 128 : h * 128 + 128, :]).astype(BF16)
             if part == 0:
@@ -424,12 +424,12 @@
             else:
                 o_all[core, rows, h * 128 : h * 128 + 128] = value
 
-    @pl.loop(0, 2)
-    def _(n):
+    o_copies = []
+    for n in range(2):
         attend(0, n)
-
-    o_copy = remote(o_send, o_all.at[core], sib_ssem.at[3], sib_rsem.at[3], sibling)
-    o_copy.start()
+        half = pl.ds(n * 128, 128)
+        o_copies.append(remote(o_send.at[half], o_all.at[core, half], sib_ssem.at[3 + n], sib_rsem.at[3 + n], sibling))
+        o_copies[n].start()
 
     @pl.loop(0, 2)
     def _(n):
@@ -437,7 +437,8 @@
 
     for copy in [*st_copies, *tot_copies, *pre_copies, *sib_copies, *started.values()]:
         copy.wait_send()
-    o_copy.wait()
+    for copy in o_copies:
+        copy.wait()
     o_ref[:, 0:512] = o_all[0]
     o_ref[:, 512:1024] = o_all[1]
 
@@ -483,7 +484,7 @@
         dma((2 * NZ - 1,)), dma((2 * NZ - 1,)),
         dma((NX - 1,)), dma((NX - 1,)),
         dma((2 * NZ - 1,)), dma((2 * NZ - 1,)),
-        dma((4,)), dma((4,)),
+        dma((5,)), dma((5,)),
         dma((2, NX - 1)), dma((2, NX - 1)),
         dma((2, 2, 4, NX)), dma((2, 2, 4, NX)),
         dma((2, 2, 4)), dma((2, 2, 4)),

time: 85.1 us -> 86.1 us (1.012)
  Pallas kernels: 83.1 us -> 84.1 us
    pallas_call x1, Pallas kernels: 83.1 us -> 84.1 us  [local(): pl.pallas_call(kernel, name='mixer_and_attention', out_shape=jax.ShapeDty...]
where the time goes in v5:
time: 86.1 us; the launch traced here: 86 us
  Pallas kernels  84.1 us (98%)
  local copies, waits for them, and re-layouts  1.87 us (2%)
    pallas_call x1, Pallas kernels, local(): pl.pallas_call(kernel, name='mixer_and_attention', out_shape=jax.ShapeDty...  84.1 us
    unnamed x1, local copies, waits for them, and re-layouts  1.87 us

profile of v5, /device:TPU:1, one launch (start us, length us, event | category | flops | bytes accessed | tf_op | source)
XLA Modules:
  0.0 86.0 jit_solution(4934843398959245460)
XLA Ops:
  0.0 84.1 %mixer_and_attention.1 = bf16[256,1024]{1,0:T(8,128)(2,1)} custom-call(s32[18,2,128]{2,1,0:T(2,128)} %bitcast.3, f32[1,1024]{1,0:T(1,128)} %bitcast.5, f32[1,2048]{1,0:T(1,128)} %bitcast.4, bf16[256,2048]{1,0:T(8,128)(2,1)} %hidden_hbm.1, bf16[256,1024]{1,0:T(8,128)(2,1)} %lq_hbm.1, bf16[256,256]{1,0:T(8,128)(2,1)} %lk_hbm.1, bf16[256,256]{1,0:T(8,128)(2,1)} %lv_hbm.1, ...), custom_call_target="tpu_custom_call" | custom-call | tf_op jit(solution)/shard_map/mixer_and_attention/pallas_call | solution.py:493
  84.1 1.9 %copy.13 = bf16[256,1024]{1,0:T(8,128)(2,1)} copy(bf16[256,1024]{1,0:T(8,128)(2,1)} %mixer_and_attention.1) | data formatting | bytes 1048576
